TPU v7x, 128 devices: a whole 4x4x4 slice. The times are simulated.
128 devices in a mesh: blk: 16 (over z, y), owner: 8 (over x, core).
Axes of the slice: x: 4, y: 4, z: 4, core: 2. Of those that a mesh axis runs over, the one named last changes fastest.
Arguments:
- small_emb: bfloat16 [16384, 4096], P(('blk', 'owner'))
- cluster_of: int32 [16384], P(('blk', 'owner')), may hold values from 0 to 2047, as said below
- big_emb: bfloat16 [32768, 4096], P(('blk', 'owner'))
Outputs:
- small_max: float32 [16384], P(('blk', 'owner'))
- big_max: float32 [32768], P(('blk', 'owner'))
Inputs may be any that keep to these rules, and one draw needn't show every extreme that they name: `cluster_of`: cluster c is owned by device c // 16 of the joined axes blk+owner. At most 2 documents of one device lie in the clusters of one owner; in every draw one owner receives exactly 2 documents from every device.
All inputs are finite; a program needn't handle non-finite values.
Results may differ from a plain program's by a relative error of at most 0.00045.
Values may be sent and summed in bfloat16 or wider, within the bound.
A program may use at most 128 MiB of HBM per device.

v0:
```python
import functools

import jax
import jax.numpy as jnp
from jax import lax
from jax.experimental import pallas as pl
from jax.experimental.pallas import tpu as pltpu
from jax.sharding import PartitionSpec as P

MESH = pl.DeviceIdType.MESH
F32 = jnp.float32
BF16 = jnp.bfloat16
CPO = 16
LANES = 128
CHUNK = 32
NC = 8
KC = 1024

HOMES = ((0, -2), (0, -1), (0, 0), (1, 1), (1, 0), (-1, 0), (1, 2), (2, -2))
E2, E1, E0, O3, O2, O1, O4, E3 = range(8)
AT_ONCE = 3
RELEASE = 4
GATE = 6
SMALL_HOPS = [(dy, dz) for dy in range(4) for dz in range(4) if (dy, dz) != (0, 0)]
NEAR_FIRST = (
    (1, 0), (3, 0), (2, 0), (0, 1), (0, 3), (1, 1), (3, 3), (1, 3), (3, 1),
    (2, 2), (0, 2), (2, 1), (1, 2), (2, 3), (3, 2),
)
X_HOPS = ((0, 1), (1, 0), (3, 1), (1, 1), (3, 0), (2, 0), (2, 1))


def pick(index, table):
    value = jnp.int32(table[0])
    for place, entry in enumerate(table[1:], 1):
        value = jnp.where(index == place, jnp.int32(entry), value)
    return value


def nt_dot(a, b):
    return lax.dot_general(a, b, (((1,), (1,)), ((), ())), preferred_element_type=F32)


def unit(values):
    values = values.astype(F32)
    inverse = lax.rsqrt(jnp.sum(values * values, axis=-1, keepdims=True) + 1e-06)
    return (values * inverse).astype(BF16)


def fold(values):
    rows, cols = values.shape
    return jnp.max(values.reshape(rows // 8, 8, cols), axis=0)


def iota(shape, dim):
    return lax.broadcasted_iota(jnp.int32, shape, dim)


def kernel(
    small_ref, cluster_ref, big_ref, small_out, big_out,
    hold, units, sbuf, rbuf, qbuf, tbuf, acc, rowacc, colacc, vsend, vbuf, wsend, wbuf, retsend, ret,
    big_ssem, big_rsem, yz_ssem, yz_rsem, x_ssem, x_rsem, v_ssem, v_rsem, w_ssem, w_rsem, ret_ssem, ret_rsem, go_sem,
):
    width = small_ref.shape[1]
    wide = width + LANES
    rows = small_ref.shape[0]
    slots = 2 * rows
    b = lax.axis_index("blk")
    o = lax.axis_index("owner")
    z, y = b // 4, b % 4
    x, core = o // 2, o % 2
    sign = 1 - 2 * core
    hub = (y + core) % 2 == 0

    def blk_at(dy, dz):
        return (z + dz + 4) % 4 * 4 + (y + dy + 4) % 4

    def turned(dy, dz):
        return {"blk": blk_at(sign * dy, dz), "owner": o}

    def row_at(dx, dc):
        return (x + dx) % 4 * 2 + (core + dc) % 2

    barrier = pltpu.get_barrier_semaphore()
    for dy, dz in SMALL_HOPS:
        pl.semaphore_signal(barrier, inc=1, device_id={"blk": blk_at(dy, dz), "owner": o}, device_id_type=MESH)
    for dx, dc in X_HOPS:
        pl.semaphore_signal(barrier, inc=1, device_id={"blk": b, "owner": row_at(dx, dc)}, device_id_type=MESH)

    cluster_lanes = jnp.broadcast_to(cluster_ref[...], (rows, rows))
    cluster_rows = jnp.transpose(cluster_lanes.astype(F32)).astype(jnp.int32)
    owner_lanes, owner_rows = cluster_lanes // CPO, cluster_rows // CPO
    earlier = (owner_lanes == owner_rows) & (iota((rows, rows), 0) < iota((rows, rows), 1))
    rank = jnp.sum(jnp.where(earlier, 1.0, 0.0), axis=0, keepdims=True).astype(jnp.int32)
    owner_of_doc = cluster_ref[...] // CPO
    slot_of_doc = owner_of_doc % 8 * 32 + owner_of_doc // 8 * 2 + rank
    place = jnp.where(iota((slots, rows), 0) == slot_of_doc, 1.0, 0.0).astype(BF16)
    label = jnp.where(iota((rows, LANES), 1) == cluster_rows % CPO, 1.0, 0.0).astype(BF16)

    @pl.loop(0, rows // 16)
    def _(step):
        at = pl.ds(pl.multiple_of(step * 16, 16), 16)
        units[at, :] = unit(small_ref[at, :])

    @pl.loop(0, width // 512)
    def _(step):
        at = pl.ds(pl.multiple_of(step * 512, 512), 512)
        sbuf[:, at] = jnp.dot(place, units[:, at], preferred_element_type=F32).astype(BF16)

    sbuf[:, pl.ds(width, LANES)] = jnp.dot(place, label, preferred_element_type=F32).astype(BF16)

    pl.semaphore_wait(barrier, len(SMALL_HOPS) + len(X_HOPS))

    def big_copy(lane, c, slot, to_slot, to):
        at = pl.ds(pl.multiple_of(c * CHUNK, CHUNK), CHUNK)
        return pltpu.make_async_remote_copy(
            src_ref=hold.at[slot, at],
            dst_ref=hold.at[to_slot, at],
            send_sem=big_ssem.at[lane, c],
            recv_sem=big_rsem.at[to_slot, c],
            device_id=turned(*to),
            device_id_type=MESH,
        )

    def own_right(c):
        return big_copy(0, c, E0, E1, (0, 1))

    def e1_right(c):
        return big_copy(1, c, E1, E2, (0, 1))

    def e2_down(c):
        return big_copy(2, c, E2, E3, (-2, 0))

    def o2_left(c):
        return big_copy(3, c, O2, O3, (0, -1))

    def o3_left(c):
        return big_copy(4, c, O3, O4, (0, -1))

    def own_up(c):
        return big_copy(0, c, E0, O1, (1, 0))

    def own_down(c):
        return big_copy(1, c, E0, O2, (-1, 0))

    def arrived(slot, c):
        big_copy(0, c, slot, slot, (0, 1)).wait_recv()

    def send_own(c):
        for part in range(CHUNK // 16):
            at = pl.ds(pl.multiple_of(c * CHUNK + part * 16, 16), 16)
            hold[E0, at, :] = unit(big_ref[at, :])

        @pl.when(hub)
        def _():
            own_right(c).start()

        @pl.when(jnp.logical_not(hub))
        def _():
            own_down(c).start()
            own_up(c).start()

    def x_copy(n):
        dx, dc = X_HOPS[n]
        to = row_at(dx, dc)
        return pltpu.make_async_remote_copy(
            src_ref=sbuf.at[pl.ds(pl.multiple_of(to * 32, 32), 32)],
            dst_ref=rbuf.at[pl.ds(pl.multiple_of(o * 32, 32), 32)],
            send_sem=x_ssem.at[n],
            recv_sem=x_rsem.at[n],
            device_id={"blk": b, "owner": to},
            device_id_type=MESH,
        )

    for n in range(7):
        x_copy(n).start()
    mine = pl.ds(pl.multiple_of(o * 32, 32), 32)
    rbuf[mine, :] = sbuf[mine, :]

    pl.loop(0, NC)(send_own)

    rowacc[...] = jnp.full(rowacc.shape, -1.0, F32)
    colacc[...] = jnp.full(colacc.shape, -1.0, F32)

    def product(m, n, left, right):
        at = (pl.ds(0, m), pl.ds(0, n))
        acc[at] = nt_dot(left(0), right(0))

        @pl.loop(1, width // KC)
        def _(k):
            acc[at] += nt_dot(left(k), right(k))

    def features(k):
        return pl.ds(pl.multiple_of(k * KC, KC), KC)

    def meet(first, count, slot, r, n):
        size = hold.shape[1]
        m = count * size
        product(
            m,
            n,
            lambda k: hold[pl.ds(first, count), :, features(k)].reshape(m, KC),
            lambda k: hold[slot, pl.ds(r, n), features(k)],
        )
        for step in range(count):
            gram = acc[pl.ds(step * size, size), pl.ds(0, n)]
            if first + step == slot:
                gram = jnp.where(iota(gram.shape, 0) == iota(gram.shape, 1) + r, -1.0, gram)
            at = pl.ds(r, n)
            colacc[slot, :, at] = jnp.maximum(colacc[slot, :, at], fold(gram))
            if first + step != slot:
                for part in range(n // LANES):
                    here = gram[:, part * LANES : (part + 1) * LANES]
                    rowacc[first + step] = jnp.maximum(rowacc[first + step], here)

    def on(role, body):
        pl.when(hub if role else jnp.logical_not(hub))(body)

    def yz_copy(n):
        dy, dz = NEAR_FIRST[n]
        to = blk_at(dy, dz)
        return pltpu.make_async_remote_copy(
            src_ref=qbuf.at[pl.ds(pl.multiple_of(to * 16, 16), 16)],
            dst_ref=tbuf.at[pl.ds(pl.multiple_of(b * 16, 16), 16)],
            send_sem=yz_ssem.at[n],
            recv_sem=yz_rsem.at[n],
            device_id={"blk": to, "owner": o},
            device_id_type=MESH,
        )

    def regroup():
        for n in range(7):
            x_copy(n).wait_recv()
        to_row = iota((slots, slots), 0)
        source = to_row % 16 // 2 * 32 + to_row // 16 * 2 + to_row % 2
        move = jnp.where(iota((slots, slots), 1) == source, 1.0, 0.0).astype(BF16)

        @pl.loop(0, width // 512)
        def _(step):
            at = pl.ds(pl.multiple_of(step * 512, 512), 512)
            qbuf[:, at] = jnp.dot(move, rbuf[:, at], preferred_element_type=F32).astype(BF16)

        tail = pl.ds(width, LANES)
        qbuf[:, tail] = jnp.dot(move, rbuf[:, tail], preferred_element_type=F32).astype(BF16)
        for n in range(AT_ONCE):
            yz_copy(n).start()
        here = pl.ds(pl.multiple_of(b * 16, 16), 16)
        tbuf[here, :] = qbuf[here, :]

    def release():
        other = {"blk": b, "owner": row_at(0, 1)}
        pl.semaphore_signal(go_sem, inc=1, device_id=other, device_id_type=MESH)
        for n in range(AT_ONCE, 15):
            yz_copy(n).start()

    def released():
        pl.semaphore_wait(go_sem, 1)
        for n in range(AT_ONCE, 15):
            yz_copy(n).start()

    def v_copy(n):
        to = blk_at(*NEAR_FIRST[n])
        return pltpu.make_async_remote_copy(
            src_ref=vsend, dst_ref=vbuf.at[b], send_sem=v_ssem.at[n], recv_sem=v_rsem.at[n],
            device_id={"blk": to, "owner": o}, device_id_type=MESH,
        )

    def w_copy(n):
        to = row_at(*X_HOPS[n])
        return pltpu.make_async_remote_copy(
            src_ref=wsend, dst_ref=wbuf.at[o], send_sem=w_ssem.at[n], recv_sem=w_rsem.at[n],
            device_id={"blk": b, "owner": to}, device_id_type=MESH,
        )

    def owner_maxima():
        for n in range(15):
            yz_copy(n).wait_recv()
        product(slots, slots, lambda k: tbuf[:, features(k)], lambda k: tbuf[:, features(k)])
        labels = tbuf[:, pl.ds(width, LANES)]
        same = nt_dot(labels, labels) > 0.5
        same = same & (iota((slots, slots), 0) != iota((slots, slots), 1))
        best = jnp.max(jnp.where(same, acc[pl.ds(0, slots), :], -1.0), axis=0, keepdims=True)
        vsend[...] = jnp.broadcast_to(best, vsend.shape)
        for n in range(15):
            v_copy(n).start()
        vbuf[b] = vsend[...]

    def pass_back():
        for n in range(15):
            v_copy(n).wait_recv()
        for group in range(2):
            packed = vbuf[group * 8]
            for other in range(1, 8):
                packed = jnp.where(iota(packed.shape, 0) == other, vbuf[group * 8 + other], packed)
            packed = pltpu.roll(packed, (16 - b) * 16 % slots, 1)
            wsend[pl.ds(group * 8, 8), :] = packed[:, :LANES]
        for n in range(7):
            w_copy(n).start()
        wbuf[o] = wsend[...]

    def small_result():
        for n in range(7):
            w_copy(n).wait_recv()
        table = wbuf[...].reshape(8 * 16, LANES)
        row_of_doc = owner_of_doc % 8 * 16 + owner_of_doc // 8
        chosen = jnp.where(iota((8 * 16, rows), 0) == row_of_doc, 1.0, 0.0)
        found = lax.dot_general(
            table, chosen, (((0,), (0,)), ((), ())), precision=lax.Precision.HIGHEST, preferred_element_type=F32
        )
        found = jnp.where(iota(found.shape, 0) == 2 * o + rank, found, 0.0)
        small_out[...] = jnp.sum(found, axis=0, keepdims=True)

    def first_steps():
        @pl.loop(0, NC)
        def _(c):
            arrived(O2, c)
            o2_left(c).start()

            @pl.when(c >= GATE)
            def _():
                arrived(E1, c - GATE)
                e1_right(c - GATE).start()

        @pl.loop(NC - GATE, NC)
        def _(c):
            arrived(E1, c)
            e1_right(c).start()

    def o3_steps():
        @pl.loop(0, NC)
        def _(c):
            arrived(O3, c)
            o3_left(c).start()

    def second_step(c, then):
        def body():
            arrived(E2, c)
            e2_down(c).start()
            if c == RELEASE:
                release()
            then()

        return body

    def wait_all(slot, start, stop):
        @pl.loop(start, stop)
        def _(c):
            arrived(slot, c)

    def half(slot, part, first, count):
        start = part * NC // 2
        if slot != E2:
            wait_all(slot, start, start + NC // 2)
        meet(first, count, slot, part * 128, 128)

    on(False, lambda: meet(E0, 1, E0, 0, 256))
    on(True, first_steps)
    regroup()
    on(True, o3_steps)
    on(True, lambda: wait_all(O1, 0, NC))
    on(True, second_step(0, lambda: meet(E1, 4, O1, 0, 256)))
    on(True, second_step(1, lambda: meet(E1, 3, O2, 0, 256)))
    on(True, second_step(2, lambda: meet(E1, 2, E0, 0, 256)))
    on(True, second_step(3, lambda: half(E2, 0, E0, 4)))
    on(True, second_step(4, lambda: half(O4, 0, O2, 2)))
    on(True, second_step(5, lambda: None))
    on(True, second_step(6, lambda: half(E3, 0, E1, 3)))
    on(True, second_step(7, lambda: half(E2, 1, E0, 4)))
    on(True, lambda: half(O4, 1, O2, 2))
    on(False, released)
    owner_maxima()

    def finish(slot):
        whole = jnp.maximum(fold(jnp.transpose(rowacc[slot])), colacc[slot])
        return jnp.broadcast_to(jnp.max(whole, axis=0, keepdims=True), whole.shape)

    def home_copy(slot):
        return pltpu.make_async_remote_copy(
            src_ref=retsend.at[slot], dst_ref=ret.at[slot], send_sem=ret_ssem.at[slot], recv_sem=ret_rsem.at[slot],
            device_id=turned(*HOMES[slot]), device_id_type=MESH,
        )

    def send_home(slots_done):
        for slot in slots_done:
            retsend[slot] = finish(slot)
            home_copy(slot).start()

    def big_result(others):
        best = finish(E0)
        for slot in others:
            home_copy(slot).wait_recv()
            best = jnp.maximum(best, ret[slot])
        big_out[...] = best[0:1]

    def last_pairs():
        send_home((O1, O2, O4))
        half(E3, 1, E2, 4)
        meet(E2, 1, E3, 0, 128)
        send_home((E3, E2, E1, O3))

    def end_hub():
        big_result((E1, E2, E3))

        for slot in (E1, E2, E3, O1, O2, O3, O4):
            home_copy(slot).wait_send()

        @pl.loop(0, NC)
        def _(c):
            own_right(c).wait_send()
            e1_right(c).wait_send()
            e2_down(c).wait_send()
            o2_left(c).wait_send()
            o3_left(c).wait_send()

    def last_relay():
        big_result((O1, O2, O3, O4))

        @pl.loop(0, NC)
        def _(c):
            own_up(c).wait_send()
            own_down(c).wait_send()

    on(True, last_pairs)
    pass_back()
    small_result()
    on(True, end_hub)
    on(False, last_relay)
    for n in range(15):
        yz_copy(n).wait_send()
        v_copy(n).wait_send()
    for n in range(7):
        x_copy(n).wait_send()
        w_copy(n).wait_send()


def body(small_emb, cluster_of, big_emb):
    rows, width = small_emb.shape
    count = big_emb.shape[0]
    wide = width + LANES
    dma = pltpu.SemaphoreType.DMA
    small_max, big_max = pl.pallas_call(
        kernel,
        out_shape=(pltpu.VMEM((1, rows), F32), pltpu.VMEM((1, count), F32)),
        in_specs=[pl.BlockSpec(memory_space=pltpu.VMEM)] * 3,
        out_specs=[pl.BlockSpec(memory_space=pltpu.VMEM)] * 2,
        scratch_shapes=[
            pltpu.VMEM((8, count, width), BF16),
            pltpu.VMEM((rows, width), BF16),
            pltpu.VMEM((2 * rows, wide), BF16),
            pltpu.VMEM((2 * rows, wide), BF16),
            pltpu.VMEM((2 * rows, wide), BF16),
            pltpu.VMEM((2 * rows, wide), BF16),
            pltpu.VMEM((4 * count, count), F32),
            pltpu.VMEM((8, count, LANES), F32),
            pltpu.VMEM((8, 8, count), F32),
            pltpu.VMEM((8, 2 * rows), F32),
            pltpu.VMEM((16, 8, 2 * rows), F32),
            pltpu.VMEM((16, LANES), F32),
            pltpu.VMEM((8, 16, LANES), F32),
            pltpu.VMEM((8, 8, count), F32),
            pltpu.VMEM((8, 8, count), F32),
            dma((5, NC)), dma((8, NC)), dma((15,)), dma((15,)), dma((7,)), dma((7,)),
            dma((15,)), dma((15,)), dma((7,)), dma((7,)), dma((8,)), dma((8,)),
            pltpu.SemaphoreType.REGULAR,
        ],
        compiler_params=pltpu.CompilerParams(
            collective_id=0, has_side_effects=True, vmem_limit_bytes=56 * 2**20
        ),
    )(small_emb, cluster_of.reshape(1, rows), big_emb)
    return jnp.maximum(small_max.reshape(rows), -1.0), jnp.maximum(big_max.reshape(count), -1.0)


def solution(mesh):
    return jax.shard_map(
        body,
        mesh=mesh,
        in_specs=(P(("blk", "owner"), None), P(("blk", "owner")), P(("blk", "owner"), None)),
        out_specs=(P(("blk", "owner")), P(("blk", "owner"))),
        check_vma=False,
    )
```

profile of v0, /device:TPU:1, one launch (start us, length us, event | category | flops | bytes accessed | tf_op | source)
XLA Modules:
  0.0 102.8 jit_solution(18048778127465519735)
XLA Ops:
  0.6 101.1 %shard_map.50 = (f32[1,128]{1,0:T(1,128)S(1)}, f32[1,256]{1,0:T(1,128)S(1)}) custom-call(bf16[128,4096]{1,0:T(8,128)(2,1)} %small_ref.1, s32[1,128]{1,0:T(1,128)} %bitcast.5, bf16[256,4096]{1,0:T(8,128)(2,1)} %big_ref.1), custom_call_target="tpu_custom_call" | custom-call | tf_op jit(solution)/shard_map/pallas_call | solution.py:440
  101.8 0.5 maximum_bitcast_fusion
  102.3 0.6 broadcast_maximum_fusion
where the time goes:
time: 103 us
  Pallas kernels  101 us (98%)
  other arithmetic  1.08 us (1%)
    pallas_call x1, Pallas kernels, body(): pl.pallas_call(kernel, out_shape=(pltpu.VMEM((1, rows), F32), pltpu.VMEM(...  101 us

commit v1 on v0

--- a/solution.py
+++ b/solution.py
@@ -18,8 +18,9 @@
 
 HOMES = ((0, -2), (0, -1), (0, 0), (1, 1), (1, 0), (-1, 0), (1, 2), (2, -2))
 E2, E1, E0, O3, O2, O1, O4, E3 = range(8)
-AT_ONCE = 3
-RELEASE = 4
+AT_ONCE = 9
+RELEASE = 5
+AHEAD = 2
 GATE = 6
 SMALL_HOPS = [(dy, dz) for dy in range(4) for dz in range(4) if (dy, dz) != (0, 0)]
 NEAR_FIRST = (
@@ -56,10 +57,15 @@
 
 
 def kernel(
-    small_ref, cluster_ref, big_ref, small_out, big_out,
+    small_hbm, cluster_ref, big_hbm, small_out, big_out,
+    small_ref, big_ref, in_sem,
     hold, units, sbuf, rbuf, qbuf, tbuf, acc, rowacc, colacc, vsend, vbuf, wsend, wbuf, retsend, ret,
     big_ssem, big_rsem, yz_ssem, yz_rsem, x_ssem, x_rsem, v_ssem, v_rsem, w_ssem, w_rsem, ret_ssem, ret_rsem, go_sem,
 ):
+    big_in = pltpu.make_async_copy(big_hbm, big_ref, in_sem.at[0])
+    small_in = pltpu.make_async_copy(small_hbm, small_ref, in_sem.at[1])
+    big_in.start()
+    small_in.start()
     width = small_ref.shape[1]
     wide = width + LANES
     rows = small_ref.shape[0]
@@ -96,19 +102,18 @@
     place = jnp.where(iota((slots, rows), 0) == slot_of_doc, 1.0, 0.0).astype(BF16)
     label = jnp.where(iota((rows, LANES), 1) == cluster_rows % CPO, 1.0, 0.0).astype(BF16)
 
-    @pl.loop(0, rows // 16)
-    def _(step):
-        at = pl.ds(pl.multiple_of(step * 16, 16), 16)
-        units[at, :] = unit(small_ref[at, :])
-
-    @pl.loop(0, width // 512)
-    def _(step):
-        at = pl.ds(pl.multiple_of(step * 512, 512), 512)
-        sbuf[:, at] = jnp.dot(place, units[:, at], preferred_element_type=F32).astype(BF16)
-
-    sbuf[:, pl.ds(width, LANES)] = jnp.dot(place, label, preferred_element_type=F32).astype(BF16)
-
-    pl.semaphore_wait(barrier, len(SMALL_HOPS) + len(X_HOPS))
+    def place_documents():
+        @pl.loop(0, rows // 16)
+        def _(step):
+            at = pl.ds(pl.multiple_of(step * 16, 16), 16)
+            units[at, :] = unit(small_ref[at, :])
+
+        @pl.loop(0, width // 512)
+        def _(step):
+            at = pl.ds(pl.multiple_of(step * 512, 512), 512)
+            sbuf[:, at] = jnp.dot(place, units[:, at], preferred_element_type=F32).astype(BF16)
+
+        sbuf[:, pl.ds(width, LANES)] = jnp.dot(place, label, preferred_element_type=F32).astype(BF16)
 
     def big_copy(lane, c, slot, to_slot, to):
         at = pl.ds(pl.multiple_of(c * CHUNK, CHUNK), CHUNK)
@@ -171,12 +176,18 @@
             device_id_type=MESH,
         )
 
+    small_in.wait()
+    soon = z < 2
+    pl.when(soon)(place_documents)
+    big_in.wait()
+    pl.semaphore_wait(barrier, len(SMALL_HOPS) + len(X_HOPS))
+    pl.loop(0, AHEAD)(send_own)
+    pl.when(jnp.logical_not(soon))(place_documents)
     for n in range(7):
         x_copy(n).start()
     mine = pl.ds(pl.multiple_of(o * 32, 32), 32)
     rbuf[mine, :] = sbuf[mine, :]
-
-    pl.loop(0, NC)(send_own)
+    pl.loop(AHEAD, NC)(send_own)
 
     rowacc[...] = jnp.full(rowacc.shape, -1.0, F32)
     colacc[...] = jnp.full(colacc.shape, -1.0, F32)
@@ -325,11 +336,14 @@
             arrived(E1, c)
             e1_right(c).start()
 
-    def o3_steps():
-        @pl.loop(0, NC)
-        def _(c):
-            arrived(O3, c)
-            o3_left(c).start()
+    def o3_steps(start, stop):
+        def body():
+            @pl.loop(start, stop)
+            def _(c):
+                arrived(O3, c)
+                o3_left(c).start()
+
+        return body
 
     def second_step(c, then):
         def body():
@@ -354,8 +368,9 @@
 
     on(False, lambda: meet(E0, 1, E0, 0, 256))
     on(True, first_steps)
+    on(True, o3_steps(0, 5))
     regroup()
-    on(True, o3_steps)
+    on(True, o3_steps(5, NC))
     on(True, lambda: wait_all(O1, 0, NC))
     on(True, second_step(0, lambda: meet(E1, 4, O1, 0, 256)))
     on(True, second_step(1, lambda: meet(E1, 3, O2, 0, 256)))
@@ -440,9 +455,12 @@
     small_max, big_max = pl.pallas_call(
         kernel,
         out_shape=(pltpu.VMEM((1, rows), F32), pltpu.VMEM((1, count), F32)),
-        in_specs=[pl.BlockSpec(memory_space=pltpu.VMEM)] * 3,
+        in_specs=[pl.BlockSpec(memory_space=space) for space in (pl.ANY, pltpu.VMEM, pl.ANY)],
         out_specs=[pl.BlockSpec(memory_space=pltpu.VMEM)] * 2,
         scratch_shapes=[
+            pltpu.VMEM((rows, width), BF16),
+            pltpu.VMEM((count, width), BF16),
+            dma((2,)),
             pltpu.VMEM((8, count, width), BF16),
             pltpu.VMEM((rows, width), BF16),
             pltpu.VMEM((2 * rows, wide), BF16),

time: 103 us -> 102 us (level)
  no operation moved by 1% of the time
where the time goes in v1:
time: 102 us
  Pallas kernels  100 us (98%)
  other arithmetic  1.08 us (1%)
    pallas_call x1, Pallas kernels, body(): pl.pallas_call(kernel, out_shape=(pltpu.VMEM((1, rows), F32), pltpu.VMEM(...  100 us

profile of v1, /device:TPU:1, one launch (start us, length us, event | category | flops | bytes accessed | tf_op | source)
XLA Modules:
  0.0 102.0 jit_solution(17120460126307243769)
XLA Ops:
  0.6 100.2 %shard_map.50 = (f32[1,128]{1,0:T(1,128)S(1)}, f32[1,256]{1,0:T(1,128)S(1)}) custom-call(bf16[128,4096]{1,0:T(8,128)(2,1)} %small_hbm.1, s32[1,128]{1,0:T(1,128)} %bitcast.5, bf16[256,4096]{1,0:T(8,128)(2,1)} %big_hbm.1), custom_call_target="tpu_custom_call" | custom-call | tf_op jit(solution)/shard_map/pallas_call | solution.py:455
  100.9 0.5 maximum_bitcast_fusion
  101.4 0.6 broadcast_maximum_fusion

commit v2 on v1

--- a/solution.py
+++ b/solution.py
@@ -19,7 +19,7 @@
 HOMES = ((0, -2), (0, -1), (0, 0), (1, 1), (1, 0), (-1, 0), (1, 2), (2, -2))
 E2, E1, E0, O3, O2, O1, O4, E3 = range(8)
 AT_ONCE = 9
-RELEASE = 5
+RELEASE = 3
 AHEAD = 2
 GATE = 6
 SMALL_HOPS = [(dy, dz) for dy in range(4) for dz in range(4) if (dy, dz) != (0, 0)]

time: 102 us -> 104 us (1.020)
  Pallas kernels: 100 us -> 102 us
    pallas_call x1, Pallas kernels: 100 us -> 102 us  [body(): pl.pallas_call(kernel, out_shape=(pltpu.VMEM((1, rows), F32), pltpu.VMEM(...]
where the time goes in v2:
time: 104 us
  Pallas kernels  102 us (98%)
  other arithmetic  1.08 us (1%)
    pallas_call x1, Pallas kernels, body(): pl.pallas_call(kernel, out_shape=(pltpu.VMEM((1, rows), F32), pltpu.VMEM(...  102 us

profile of v2, /device:TPU:1, one launch (start us, length us, event | category | flops | bytes accessed | tf_op | source)
XLA Modules:
  0.0 103.6 jit_solution(13849546335632191945)
XLA Ops:
  0.6 101.9 %shard_map.50 = (f32[1,128]{1,0:T(1,128)S(1)}, f32[1,256]{1,0:T(1,128)S(1)}) custom-call(bf16[128,4096]{1,0:T(8,128)(2,1)} %small_hbm.1, s32[1,128]{1,0:T(1,128)} %bitcast.5, bf16[256,4096]{1,0:T(8,128)(2,1)} %big_hbm.1), custom_call_target="tpu_custom_call" | custom-call | tf_op jit(solution)/shard_map/pallas_call | solution.py:455
  102.5 0.5 maximum_bitcast_fusion
  103.0 0.6 broadcast_maximum_fusion
